TPU v7x, 32 devices: a whole 2x2x4 slice. The times are simulated.
32 devices in a mesh: dp: 8 (over y, x, core), stream: 4 (over z).
Axes of the slice: x: 2, y: 2, z: 4, core: 2. Of those that a mesh axis runs over, the one named last changes fastest.
Arguments:
- tokens: bfloat16 [2, 8, 4, 591, 768], P(None, 'dp', 'stream'), may hold values from -6 to 6
- text_lengths: int32 [2, 8, 24], P(None, 'dp'), may hold values from 1 to 40, 591 in all within a row
- pair_text: int32 [2, 8, 9], P(None, 'dp'), may hold values from -1 to 23, as said below
- ln1_gain: bfloat16 [768], replicated, may hold values from 0.099609375 to 1.8984375
- ln1_bias: bfloat16 [768], replicated, may hold values from -1.75 to 1.75
- w_qkv: bfloat16 [768, 2304], replicated, may hold values from -0.3125 to 0.3125
- q_bias: bfloat16 [768], replicated, may hold values from -1.75 to 1.75
- v_bias: bfloat16 [768], replicated, may hold values from -0.625 to 0.625
- w_out: bfloat16 [768, 768], replicated, may hold values from -1.25 to 1.25
- ln2_gain: bfloat16 [768], replicated, may hold values from 0.099609375 to 1.8984375
- ln2_bias: bfloat16 [768], replicated, may hold values from -1.75 to 1.75
- vis_up: bfloat16 [768, 3072], replicated, may hold values from -0.21875 to 0.21875
- vis_down: bfloat16 [3072, 768], replicated, may hold values from -0.21875 to 0.21875
- vis_bias: bfloat16 [768], replicated, may hold values from -1.75 to 1.75
- txt_up: bfloat16 [768, 3072], replicated, may hold values from -0.21875 to 0.21875
- txt_down: bfloat16 [3072, 768], replicated, may hold values from -0.21875 to 0.21875
- txt_bias: bfloat16 [768], replicated, may hold values from -1.75 to 1.75
- cotangent: bfloat16 [2, 8, 4, 591, 768], P(None, 'dp', 'stream'), may hold values from -6 to 6
Outputs:
- output: bfloat16 [2, 8, 4, 591, 768], P(None, 'dp', 'stream')
- tokens_grad: bfloat16 [2, 8, 4, 591, 768], P(None, 'dp', 'stream')
- ln1_gain_grad: float32 [768], P('dp')
- ln1_bias_grad: float32 [768], P('dp')
- w_qkv_grad: float32 [768, 2304], P('dp', 'stream')
- q_bias_grad: float32 [768], P('dp')
- v_bias_grad: float32 [768], P('dp')
- w_out_grad: float32 [768, 768], P('dp', 'stream')
- ln2_gain_grad: float32 [768], P('dp')
- ln2_bias_grad: float32 [768], P('dp')
- vis_up_grad: float32 [768, 3072], P('dp', 'stream')
- vis_down_grad: float32 [3072, 768], P('dp', 'stream')
- vis_bias_grad: float32 [768], P('dp')
- txt_up_grad: float32 [768, 3072], P('dp', 'stream')
- txt_down_grad: float32 [3072, 768], P('dp', 'stream')
- txt_bias_grad: float32 [768], P('dp')
Inputs may be any that keep to these rules, and one draw needn't show every extreme that they name: `text_lengths`: the text lengths of a group sum to 591. `pair_text`: no text item is named twice in a group; in each image block exactly 2 of its 3 images are paired, the others hold -1.
All inputs are finite; a program needn't handle non-finite values.
Results may differ from a plain program's by a relative error of at most 0.015.
Values may be sent and summed in bfloat16 or wider, within the bound.
A program may use at most 576 MiB of HBM per device.

v0:
```python
import jax
import jax.numpy as jnp
from jax import lax
from jax.sharding import PartitionSpec as P

HEADS = 12
PATCHES = 197


EPSILON = 1e-06
MASKED = -1e30
ROOT_HALF = 0.7071067811865476
ROOT_TWO_PI = 0.3989422804014327


def layer_norm(values, norm_gain, norm_bias):
    centred = values - jnp.mean(values, axis=-1, keepdims=True)
    inverse = lax.rsqrt(jnp.mean(centred * centred, axis=-1, keepdims=True) + EPSILON)
    normed = centred * inverse
    return (normed * norm_gain + norm_bias, normed, inverse)


def norm_back(grad_out, normed, inverse, norm_gain):
    scaled = grad_out * norm_gain
    grad_in = inverse * (
        scaled
        - jnp.mean(scaled, axis=-1, keepdims=True)
        - normed * jnp.mean(scaled * normed, axis=-1, keepdims=True)
    )
    return (grad_in, jnp.sum(grad_out * normed, axis=0), jnp.sum(grad_out, axis=0))


def row_dot(left, right):
    return lax.dot_general(
        left, right, (((0,), (0,)), ((), ())), preferred_element_type=jnp.float32
    )


def right_dot(left, right):
    return lax.dot_general(
        left, right, (((1,), (1,)), ((), ())), preferred_element_type=jnp.float32
    )


def gelu_slope(up_val):
    return (
        0.5 * (1.0 + lax.erf(up_val * ROOT_HALF))
        + up_val * jnp.exp(-0.5 * up_val * up_val) * ROOT_TWO_PI
    )


def sequence_ids(lengths, pairs, row_count, patches):
    item_count = lengths.shape[0]
    image_count = pairs.shape[0]
    image_ids = jnp.arange(3 * row_count, dtype=jnp.int32) // patches
    finish = jnp.cumsum(lengths)
    starts = finish - lengths
    places = jnp.arange(row_count, dtype=jnp.int32)[:, None]
    member = (places >= starts[None, :]) & (places < finish[None, :])
    numbers = jnp.arange(item_count, dtype=jnp.int32)
    paired_with = pairs[:, None] == numbers[None, :]
    partner = jnp.sum(
        jnp.where(paired_with, jnp.arange(image_count, dtype=jnp.int32)[:, None], 0), axis=0
    )
    text_seq = jnp.where(jnp.any(paired_with, axis=0), partner, image_count + numbers)
    text_ids = jnp.sum(jnp.where(member, text_seq[None, :], 0), axis=1)
    return jnp.concatenate([image_ids, text_ids])


def attention_scores(queries, key_heads, allowed, scale):
    raw = jnp.einsum("qhe,khe->hqk", queries, key_heads, preferred_element_type=jnp.float32) * scale
    return jnp.where(allowed[None], raw, MASKED)


def reduce_items(grads):
    vectors, grad_qkv, grad_out, grad_vup, grad_vdown, grad_tup, grad_tdown = grads
    return (
        lax.psum_scatter(vectors, "dp", scatter_dimension=0, tiled=True),
        lax.psum_scatter(grad_qkv, "dp", scatter_dimension=0, tiled=True),
        lax.psum_scatter(grad_out, "dp", scatter_dimension=0, tiled=True),
        lax.psum_scatter(grad_vup, "dp", scatter_dimension=0, tiled=True),
        lax.psum_scatter(grad_vdown, "dp", scatter_dimension=0, tiled=True),
        lax.psum_scatter(grad_tup, "dp", scatter_dimension=0, tiled=True),
        lax.psum_scatter(grad_tdown, "dp", scatter_dimension=0, tiled=True),
    )


def shards(
    tokens,
    text_lengths,
    pair_text,
    ln1_gain,
    ln1_bias,
    w_qkv,
    q_bias,
    v_bias,
    w_out,
    ln2_gain,
    ln2_bias,
    vis_up,
    vis_down,
    vis_bias,
    txt_up,
    txt_down,
    txt_bias,
    cotangent,
):
    row_count = tokens.shape[3]
    width = tokens.shape[4]
    head_size = width // HEADS
    scale = head_size ** (-0.5)
    stream_pos = lax.axis_index("stream")
    is_text = stream_pos == 3
    gain1 = ln1_gain.astype(jnp.float32)
    shift1 = ln1_bias.astype(jnp.float32)
    gain2 = ln2_gain.astype(jnp.float32)
    shift2 = ln2_bias.astype(jnp.float32)
    qkv_shift = jnp.concatenate(
        [q_bias.astype(jnp.float32), jnp.zeros((width,), jnp.float32), v_bias.astype(jnp.float32)]
    )

    def micro_step(block_in, block_cot, lengths, pairs):
        seq_ids = sequence_ids(lengths, pairs, row_count, PATCHES)
        own_ids = lax.dynamic_slice_in_dim(seq_ids, stream_pos * row_count, row_count)
        values = block_in.astype(jnp.float32)
        normed1_out, normed1, inverse1 = layer_norm(values, gain1, shift1)
        hidden1 = normed1_out.astype(jnp.bfloat16)
        qkv_low = (jnp.dot(hidden1, w_qkv, preferred_element_type=jnp.float32) + qkv_shift).astype(
            jnp.bfloat16
        )
        queries = qkv_low[:, :width].reshape(row_count, HEADS, head_size)
        key_part = qkv_low[:, width : 2 * width]
        value_part = qkv_low[:, 2 * width :]
        all_keys, all_values = (
            lax.all_gather(key_part, "stream", axis=0, tiled=True),
            lax.all_gather(value_part, "stream", axis=0, tiled=True),
        )
        allowed = own_ids[:, None] == seq_ids[None, :]
        key_heads = all_keys.reshape(-1, HEADS, head_size)
        value_heads = all_values.reshape(-1, HEADS, head_size)
        scores = attention_scores(queries, key_heads, allowed, scale)
        top = jnp.max(scores, axis=-1, keepdims=True)
        expo = jnp.exp(scores - top)
        total = jnp.sum(expo, axis=-1, keepdims=True)
        probs = expo / total
        log_total = top + jnp.log(total)
        attended = jnp.einsum(
            "hqk,khe->qhe",
            probs.astype(jnp.bfloat16),
            value_heads,
            preferred_element_type=jnp.float32,
        ).reshape(row_count, width)
        attended_low = attended.astype(jnp.bfloat16)
        middle = values + jnp.dot(attended_low, w_out, preferred_element_type=jnp.float32)
        normed2_out, normed2, inverse2 = layer_norm(middle, gain2, shift2)
        hidden2 = normed2_out.astype(jnp.bfloat16)

        def run_expert(up_w, down_w, bias_w):
            up_val = jnp.dot(hidden2, up_w, preferred_element_type=jnp.float32)
            activ = jax.nn.gelu(up_val, approximate=False).astype(jnp.bfloat16)
            result = jnp.dot(activ, down_w, preferred_element_type=jnp.float32) + bias_w.astype(
                jnp.float32
            )
            grad_up = (right_dot(block_cot, down_w) * gelu_slope(up_val)).astype(jnp.bfloat16)
            grad_hidden2 = right_dot(grad_up, up_w)
            return (
                result,
                grad_hidden2,
                row_dot(hidden2, grad_up),
                row_dot(activ, block_cot),
                jnp.sum(block_cot.astype(jnp.float32), axis=0),
            )

        def vision_branch():
            parts = run_expert(vis_up, vis_down, vis_bias)
            return parts + (
                jnp.zeros_like(parts[2]),
                jnp.zeros_like(parts[3]),
                jnp.zeros_like(parts[4]),
            )

        def text_branch():
            parts = run_expert(txt_up, txt_down, txt_bias)
            return (
                parts[0],
                parts[1],
                jnp.zeros_like(parts[2]),
                jnp.zeros_like(parts[3]),
                jnp.zeros_like(parts[4]),
                parts[2],
                parts[3],
                parts[4],
            )

        (
            expert_out,
            grad_hidden2,
            grad_vup,
            grad_vdown,
            grad_vbias,
            grad_tup,
            grad_tdown,
            grad_tbias,
        ) = lax.cond(is_text, text_branch, vision_branch)
        output_block = (middle + expert_out).astype(jnp.bfloat16)
        norm2_back, grad_gain2, grad_shift2 = norm_back(grad_hidden2, normed2, inverse2, gain2)
        grad_middle = block_cot.astype(jnp.float32) + norm2_back
        grad_branch = grad_middle.astype(jnp.bfloat16)
        grad_w_out = row_dot(attended_low, grad_branch)
        grad_attended = (
            right_dot(grad_branch, w_out).astype(jnp.bfloat16).reshape(row_count, HEADS, head_size)
        )
        probs_back = jnp.exp(attention_scores(queries, key_heads, allowed, scale) - log_total)
        grad_values = jnp.einsum(
            "hqk,qhe->khe",
            probs_back.astype(jnp.bfloat16),
            grad_attended,
            preferred_element_type=jnp.float32,
        )
        grad_probs = jnp.einsum(
            "qhe,khe->hqk", grad_attended, value_heads, preferred_element_type=jnp.float32
        )
        inner = jnp.sum(probs_back * grad_probs, axis=-1, keepdims=True)
        grad_scores = (probs_back * (grad_probs - inner)).astype(jnp.bfloat16)
        grad_queries = (
            jnp.einsum("hqk,khe->qhe", grad_scores, key_heads, preferred_element_type=jnp.float32)
            * scale
        )
        grad_keys = (
            jnp.einsum("hqk,qhe->khe", grad_scores, queries, preferred_element_type=jnp.float32)
            * scale
        )
        grad_keys = grad_keys.reshape(-1, width)
        grad_values = grad_values.reshape(-1, width)
        own_keys, own_values = (
            lax.psum_scatter(
                grad_keys.astype(jnp.bfloat16), "stream", scatter_dimension=0, tiled=True
            ).astype(jnp.float32),
            lax.psum_scatter(
                grad_values.astype(jnp.bfloat16), "stream", scatter_dimension=0, tiled=True
            ).astype(jnp.float32),
        )
        grad_qkv = jnp.concatenate(
            [grad_queries.reshape(row_count, width), own_keys, own_values], axis=1
        ).astype(jnp.bfloat16)
        grad_qkv_wide = grad_qkv.astype(jnp.float32)
        grad_qbias = jnp.sum(grad_qkv_wide[:, :width], axis=0)
        grad_vbias_attn = jnp.sum(grad_qkv_wide[:, 2 * width :], axis=0)
        grad_w_qkv = row_dot(hidden1, grad_qkv)
        grad_hidden1 = right_dot(grad_qkv, w_qkv)
        norm1_back, grad_gain1, grad_shift1 = norm_back(grad_hidden1, normed1, inverse1, gain1)
        grad_block = (grad_middle + norm1_back).astype(jnp.bfloat16)
        vectors = jnp.stack(
            [
                grad_gain1,
                grad_shift1,
                grad_qbias,
                grad_vbias_attn,
                grad_gain2,
                grad_shift2,
                grad_vbias,
                grad_tbias,
            ],
            axis=1,
        )
        grads = (vectors, grad_w_qkv, grad_w_out, grad_vup, grad_vdown, grad_tup, grad_tdown)
        return (output_block, grad_block, grads)

    def step_fn(carry, inputs):
        block_in, block_cot, lengths, pairs = inputs
        output_block, grad_block, grads = micro_step(block_in, block_cot, lengths, pairs)
        carry = jax.tree.map(jnp.add, carry, grads)
        return (carry, (output_block, grad_block))

    pieces = 1
    ff_width = vis_up.shape[1]
    initial = (
        jnp.zeros((width // pieces, 8), jnp.float32),
        jnp.zeros((width // pieces, 3 * width), jnp.float32),
        jnp.zeros((width // pieces, width), jnp.float32),
        jnp.zeros((width // pieces, ff_width), jnp.float32),
        jnp.zeros((ff_width // pieces, width), jnp.float32),
        jnp.zeros((width // pieces, ff_width), jnp.float32),
        jnp.zeros((ff_width // pieces, width), jnp.float32),
    )
    carry, stacked = lax.scan(
        step_fn, initial, (tokens[:, 0, 0], cotangent[:, 0, 0], text_lengths[:, 0], pair_text[:, 0])
    )
    totals = reduce_items(carry)
    (
        vectors,
        grad_qkv_sum,
        grad_out_sum,
        grad_vup_sum,
        grad_vdown_sum,
        grad_tup_sum,
        grad_tdown_sum,
    ) = totals
    vectors = lax.psum(vectors, "stream")
    grad_qkv_sum, grad_out_sum, grad_vup_sum, grad_vdown_sum, grad_tup_sum, grad_tdown_sum = (
        lax.psum_scatter(
            grad_qkv_sum.astype(jnp.bfloat16), "stream", scatter_dimension=1, tiled=True
        ).astype(jnp.float32),
        lax.psum_scatter(
            grad_out_sum.astype(jnp.bfloat16), "stream", scatter_dimension=1, tiled=True
        ).astype(jnp.float32),
        lax.psum_scatter(
            grad_vup_sum.astype(jnp.bfloat16), "stream", scatter_dimension=1, tiled=True
        ).astype(jnp.float32),
        lax.psum_scatter(
            grad_vdown_sum.astype(jnp.bfloat16), "stream", scatter_dimension=1, tiled=True
        ).astype(jnp.float32),
        lax.psum_scatter(
            grad_tup_sum.astype(jnp.bfloat16), "stream", scatter_dimension=1, tiled=True
        ).astype(jnp.float32),
        lax.psum_scatter(
            grad_tdown_sum.astype(jnp.bfloat16), "stream", scatter_dimension=1, tiled=True
        ).astype(jnp.float32),
    )
    output_blocks, grad_blocks = stacked
    return (
        output_blocks.reshape(tokens.shape),
        grad_blocks.reshape(tokens.shape),
        vectors[:, 0],
        vectors[:, 1],
        grad_qkv_sum,
        vectors[:, 2],
        vectors[:, 3],
        grad_out_sum,
        vectors[:, 4],
        vectors[:, 5],
        grad_vup_sum,
        grad_vdown_sum,
        vectors[:, 6],
        grad_tup_sum,
        grad_tdown_sum,
        vectors[:, 7],
    )


def solution(mesh):
    in_specs = (
        P(None, "dp", "stream", None, None),
        P(None, "dp", None),
        P(None, "dp", None),
        P(),
        P(),
        P(),
        P(),
        P(),
        P(),
        P(),
        P(),
        P(),
        P(),
        P(),
        P(),
        P(),
        P(),
        P(None, "dp", "stream", None, None),
    )
    out_specs = (
        P(None, "dp", "stream", None, None),
        P(None, "dp", "stream", None, None),
        P("dp"),
        P("dp"),
        P("dp", "stream"),
        P("dp"),
        P("dp"),
        P("dp", "stream"),
        P("dp"),
        P("dp"),
        P("dp", "stream"),
        P("dp", "stream"),
        P("dp"),
        P("dp", "stream"),
        P("dp", "stream"),
        P("dp"),
    )
    return jax.shard_map(shards, mesh=mesh, in_specs=in_specs, out_specs=out_specs, check_vma=False)
```

profile of v0, /device:TPU:0, one launch (start us, length us, event | category | flops | bytes accessed | tf_op | source)
XLA Modules:
  0.0 2151.8 jit_solution(9780913975994576826)
XLA Ops:
  19.5 1517.1 %while.29 = (s32[]{:T(128)}, f32[768,8]{0,1:T(8,128)}, f32[768,2304]{1,0:T(8,128)}, f32[768,768]{1,0:T(8,128)}, f32[768,3072]{0,1:T(8,128)}, /*index=5*/f32[3072...) while((s32[]{:T(128)}, f32[768,8]{0,1:T(8,128)}, ...), condition=%wide.region_29.30_spmd.clone, body=%wide.region_0.29_spmd.clone.sunk | while | flops 38492958720 | bytes 1323554816 | solution.py:286
  37.6 65.5 %all-gather.13.cloned.1.call-done = bf16[4,591,768]{2,1,0:T(8,128)(2,1)} async-done(((bf16[1,591,768]{2,1,0:T(8,128)(2,1)}), bf16[4,591,768]{2,1,0:T(8,128)(2,1)}) %all-gather.13.cloned.1.call-update) | async-done | bytes 3631120 | tf_op jit(solution)/shard_map/while/body/eval_jaxpr/all_gather | solution.py:135
  118.6 56.4 %all-gather.11.cloned.1.call-done = bf16[4,591,768]{2,1,0:T(8,128)(2,1)} async-done(((bf16[1,591,768]{2,1,0:T(8,128)(2,1)}), bf16[4,591,768]{2,1,0:T(8,128)(2,1)}) %all-gather.11.cloned.1.call-update) | async-done | bytes 3631120 | tf_op jit(solution)/shard_map/while/body/eval_jaxpr/all_gather | solution.py:136
  190.4 26.8 %fusion.187 = (f32[12,591]{1,0:T(8,128)S(1)}, f32[12,591,2364]{2,1,0:T(8,128)}) fusion(bf16[591,12,64]{0,2,1:T(8,128)(2,1)S(1)} %bitcast.246, bf16[2364,12,64]{0,2,1:T(8,128)(2,1)} %reshape.243, pred[591,2364]{1,0:T(8,128)(4,1)S(1)} %broadcast_compare_fusion.2), kind=kOutput, calls=%fused_computation.176.clone.1 | convolution fusion | flops 2196271616 | bytes 73026320 | tf_op jit(solution)/shard_map/while/body/eval_jaxpr/qhe,khe->hqk/dot_general | solution.py:71
  271.2 58.4 %conditional.3 = (f32[591,768]{1,0:T(8,128)S(1)}, f32[591,768]{1,0:T(8,128)S(1)}, f32[768,3072]{0,1:T(8,128)S(1)}, f32[3072,768]{1,0:T(8,128)S(1)}, f32[768,3072...) conditional(s32[]{:T(128)} %convert_element_type.384, ...), branch_computations={%region_11.13_spmd, %region_14.16_spmd} | conditional | flops 16870109184 | bytes 179543232 | solution.py:204
  341.8 26.6 %fusion.191 = bf16[12,64,2364]{2,1,0:T(8,128)(2,1)} fusion(bf16[591,12,64]{0,2,1:T(8,128)(2,1)S(1)} %bitcast.244, f32[12,591,2364]{2,1,0:T(8,128)} %get-tuple-element.889, f32[12,591]{1,0:T(8,128)S(1)} %copy-done.8), kind=kOutput, calls=%fused_computation.76.clone.1 | convolution fusion | flops 2181328896 | bytes 71629200 | tf_op jit(solution)/shard_map/while/body/eval_jaxpr/hqk,qhe->khe/dot_general | solution.py:214
  368.3 44.5 %multiply_reduce_fusion.11 = (f32[12,591]{1,0:T(8,128)S(1)}, f32[12,591,2364]{2,1,0:T(8,128)}) fusion(f32[12,591,2364]{2,1,0:T(8,128)} %get-tuple-element.889, f32[12,591]{1,0:T(8,128)S(1)} %copy-done.8, bf16[591,12,64]{0,2,1:T(8,128)(2,1)S(1)} %bitcast.245, bf16[2364,12,64]{0,2,1:T(8,128)(2,1)} %reshape.242), kind=kOutput, calls=%fused_computation.59.clone.1 | convolution fusion | flops 2196271616 | bytes 138719520 | tf_op jit(solution)/shard_map/while/body/eval_jaxpr/qhe,khe->hqk/dot_general | solution.py:220
  412.8 54.7 %multiply_convert_fusion.6 = bf16[12,591,2364]{2,1,0:T(8,128)(2,1)} fusion(f32[12,591,2364]{2,1,0:T(8,128)} %get-tuple-element.898, f32[12,591,2364]{2,1,0:T(8,128)} %get-tuple-element.889, f32[12,591]{1,0:T(8,128)S(1)} %get-tuple-element.899, f32[12,591]{1,0:T(8,128)S(1)} %copy-done.8), kind=kLoop, calls=%fused_computation.58.clone.1 | loop fusion | flops 67061952 | bytes 167711616 | tf_op jit(solution)/shard_map/while/body/eval_jaxpr/convert_element_type | solution.py:224
  541.4 211.5 %all-reduce.7.cloned.1.call-done = (bf16[2364,768]{0,1:T(8,128)(2,1)}, bf16[2364,768]{0,1:T(8,128)(2,1)}) async-done(((bf16[2364,768]{0,1:T(8,128)(2,1)}, bf16[2364,768]{0,1:T(8,128)(2,1)}), (bf16[2364,768]{0,1:T(8,128)(2,1)}, bf16[2364,768]{0,1:T(8,128)(2,1)})) %all-reduce.7.cloned.1.call-update) | async-done | bytes 7262224 | tf_op jit(solution)/shard_map/while
  794.3 62.2 %all-gather.13.cloned.1.call-done = bf16[4,591,768]{2,1,0:T(8,128)(2,1)} async-done(((bf16[1,591,768]{2,1,0:T(8,128)(2,1)}), bf16[4,591,768]{2,1,0:T(8,128)(2,1)}) %all-gather.13.cloned.1.call-update) | async-done | bytes 3631120 | tf_op jit(solution)/shard_map/while/body/eval_jaxpr/all_gather | solution.py:135
  872.0 56.3 %all-gather.11.cloned.1.call-done = bf16[4,591,768]{2,1,0:T(8,128)(2,1)} async-done(((bf16[1,591,768]{2,1,0:T(8,128)(2,1)}), bf16[4,591,768]{2,1,0:T(8,128)(2,1)}) %all-gather.11.cloned.1.call-update) | async-done | bytes 3631120 | tf_op jit(solution)/shard_map/while/body/eval_jaxpr/all_gather | solution.py:136
  943.6 26.8 %fusion.187 = (f32[12,591]{1,0:T(8,128)S(1)}, f32[12,591,2364]{2,1,0:T(8,128)}) fusion(bf16[591,12,64]{0,2,1:T(8,128)(2,1)S(1)} %bitcast.246, bf16[2364,12,64]{0,2,1:T(8,128)(2,1)} %reshape.243, pred[591,2364]{1,0:T(8,128)(4,1)S(1)} %broadcast_compare_fusion.2), kind=kOutput, calls=%fused_computation.176.clone.1 | convolution fusion | flops 2196271616 | bytes 73026320 | tf_op jit(solution)/shard_map/while/body/eval_jaxpr/qhe,khe->hqk/dot_general | solution.py:71
  993.4 25.9 %fusion.189 = bf16[12,64,591]{2,1,0:T(8,128)(2,1)S(1)} fusion(bf16[2364,12,64]{0,2,1:T(8,128)(2,1)} %reshape.242, f32[12,591,2364]{2,1,0:T(8,128)} %get-tuple-element.889, f32[12,591]{1,0:T(8,128)S(1)} %fusion.188, f32[12,591]{1,0:T(8,128)S(1)} %get-tuple-element.890), kind=kOutput, calls=%fused_computation.111.clone.1 | convolution fusion | flops 2196732928 | bytes 71657568 | tf_op jit(solution)/shard_map/while/body/eval_jaxpr/hqk,khe->qhe/dot_general | solution.py:147
  1024.7 58.2 %conditional.3 = (f32[591,768]{1,0:T(8,128)S(1)}, f32[591,768]{1,0:T(8,128)S(1)}, f32[768,3072]{0,1:T(8,128)S(1)}, f32[3072,768]{1,0:T(8,128)S(1)}, f32[768,3072...) conditional(s32[]{:T(128)} %convert_element_type.384, ...), branch_computations={%region_11.13_spmd, %region_14.16_spmd} | conditional | flops 16870109184 | bytes 179543232 | solution.py:204
  1095.1 26.6 %fusion.191 = bf16[12,64,2364]{2,1,0:T(8,128)(2,1)} fusion(bf16[591,12,64]{0,2,1:T(8,128)(2,1)S(1)} %bitcast.244, f32[12,591,2364]{2,1,0:T(8,128)} %get-tuple-element.889, f32[12,591]{1,0:T(8,128)S(1)} %copy-done.8), kind=kOutput, calls=%fused_computation.76.clone.1 | convolution fusion | flops 2181328896 | bytes 71629200 | tf_op jit(solution)/shard_map/while/body/eval_jaxpr/hqk,qhe->khe/dot_general | solution.py:214
  1121.7 44.5 %multiply_reduce_fusion.11 = (f32[12,591]{1,0:T(8,128)S(1)}, f32[12,591,2364]{2,1,0:T(8,128)}) fusion(f32[12,591,2364]{2,1,0:T(8,128)} %get-tuple-element.889, f32[12,591]{1,0:T(8,128)S(1)} %copy-done.8, bf16[591,12,64]{0,2,1:T(8,128)(2,1)S(1)} %bitcast.245, bf16[2364,12,64]{0,2,1:T(8,128)(2,1)} %reshape.242), kind=kOutput, calls=%fused_computation.59.clone.1 | convolution fusion | flops 2196271616 | bytes 138719520 | tf_op jit(solution)/shard_map/while/body/eval_jaxpr/qhe,khe->hqk/dot_general | solution.py:220
  1166.2 54.7 %multiply_convert_fusion.6 = bf16[12,591,2364]{2,1,0:T(8,128)(2,1)} fusion(f32[12,591,2364]{2,1,0:T(8,128)} %get-tuple-element.898, f32[12,591,2364]{2,1,0:T(8,128)} %get-tuple-element.889, f32[12,591]{1,0:T(8,128)S(1)} %get-tuple-element.899, f32[12,591]{1,0:T(8,128)S(1)} %copy-done.8), kind=kLoop, calls=%fused_computation.58.clone.1 | loop fusion | flops 67061952 | bytes 167711616 | tf_op jit(solution)/shard_map/while/body/eval_jaxpr/convert_element_type | solution.py:224
  1306.2 200.9 %all-reduce.7.cloned.1.call-done = (bf16[2364,768]{0,1:T(8,128)(2,1)}, bf16[2364,768]{0,1:T(8,128)(2,1)}) async-done(((bf16[2364,768]{0,1:T(8,128)(2,1)}, bf16[2364,768]{0,1:T(8,128)(2,1)}), (bf16[2364,768]{0,1:T(8,128)(2,1)}, bf16[2364,768]{0,1:T(8,128)(2,1)})) %all-reduce.7.cloned.1.call-update) | async-done | bytes 7262224 | tf_op jit(solution)/shard_map/while
  1583.5 67.3 %reduce-scatter.22.cloned.1.call-done = f32[96,2304]{1,0:T(8,128)} async-done(((f32[768,2304]{1,0:T(8,128)}), f32[96,2304]{1,0:T(8,128)}) %reduce-scatter.22.cloned.1.call-update) | async-done | bytes 884752 | tf_op jit(solution)/shard_map/reduce_scatter | solution.py:79
  1653.2 77.3 %reduce-scatter.34.cloned.1.call-done = f32[96,3072]{1,0:T(8,128)} async-done(((f32[768,3072]{1,0:T(8,128)}), f32[96,3072]{1,0:T(8,128)}) %reduce-scatter.34.cloned.1.call-update) | async-done | bytes 1179664 | tf_op jit(solution)/shard_map/reduce_scatter | solution.py:83
  1732.7 77.6 %reduce-scatter.26.cloned.1.call-done = f32[96,3072]{1,0:T(8,128)} async-done(((f32[768,3072]{1,0:T(8,128)}), f32[96,3072]{1,0:T(8,128)}) %reduce-scatter.26.cloned.1.call-update) | async-done | bytes 1179664 | tf_op jit(solution)/shard_map/reduce_scatter | solution.py:81
  1812.6 77.6 %reduce-scatter.30.cloned.1.call-done = f32[384,768]{0,1:T(8,128)} async-done(((f32[3072,768]{0,1:T(8,128)}), f32[384,768]{0,1:T(8,128)}) %reduce-scatter.30.cloned.1.call-update) | async-done | bytes 1179664 | tf_op jit(solution)/shard_map/reduce_scatter | solution.py:82
  1892.4 77.6 %reduce-scatter.38.cloned.1.call-done = f32[384,768]{0,1:T(8,128)} async-done(((f32[3072,768]{0,1:T(8,128)}), f32[384,768]{0,1:T(8,128)}) %reduce-scatter.38.cloned.1.call-update) | async-done | bytes 1179664 | tf_op jit(solution)/shard_map/reduce_scatter | solution.py:84
  1979.0 27.8 %reduce-scatter.42.cloned.1.call-done = f32[96,8]{1,0:T(8,128)} async-done(((f32[768,8]{1,0:T(8,128)}), f32[96,8]{1,0:T(8,128)}) %reduce-scatter.42.cloned.1.call-update) | async-done | bytes 3088
  (391 shorter events, 720.8 us)
Async XLA Ops:
  19.5 83.6 %all-gather.13.cloned.1.call-start = ((), (), s32[]{:S(2)}) async-start(), calls=%async_computation.27 | async-start | bytes 4546560 | tf_op jit(solution)/shard_map/while/body/eval_jaxpr/all_gather | solution.py:135
  28.7 146.3 %all-gather.11.cloned.1.call-start = ((), (), s32[]{:S(2)}) async-start(), calls=%async_computation.26 | async-start | bytes 4546560 | tf_op jit(solution)/shard_map/while/body/eval_jaxpr/all_gather | solution.py:136
  29.4 723.5 %all-reduce.7.cloned.1.call-start = ((), (), s32[]{:S(2)}) async-start(), calls=%async_computation.28 | async-start | bytes 14942208 | tf_op jit(solution)/shard_map/while
  524.1 232.2 %copy-start.19 = (f32[591]{0:T(1024)S(1)}, f32[591]{0:T(1024)}, u32[]{:S(2)}) copy-start(f32[591]{0:T(1024)} %copy-done.18) | copy-start | bytes 7096 | tf_op jit(solution)/shard_map/while
  524.1 232.3 %copy-start.24 = (f32[591]{0:T(1024)S(1)}, f32[591]{0:T(1024)}, u32[]{:S(2)}) copy-start(f32[591]{0:T(1024)} %copy-done.23) | copy-start | bytes 7096 | tf_op jit(solution)/shard_map/while
  776.6 79.9 %all-gather.13.cloned.1.call-start = ((), (), s32[]{:S(2)}) async-start(), calls=%async_computation.27 | async-start | bytes 4546560 | tf_op jit(solution)/shard_map/while/body/eval_jaxpr/all_gather | solution.py:135
  785.9 142.4 %all-gather.11.cloned.1.call-start = ((), (), s32[]{:S(2)}) async-start(), calls=%async_computation.26 | async-start | bytes 4546560 | tf_op jit(solution)/shard_map/while/body/eval_jaxpr/all_gather | solution.py:136
  786.5 720.6 %all-reduce.7.cloned.1.call-start = ((), (), s32[]{:S(2)}) async-start(), calls=%async_computation.28 | async-start | bytes 14942208 | tf_op jit(solution)/shard_map/while
  1289.2 221.4 %copy-start.19 = (f32[591]{0:T(1024)S(1)}, f32[591]{0:T(1024)}, u32[]{:S(2)}) copy-start(f32[591]{0:T(1024)} %copy-done.18) | copy-start | bytes 7096 | tf_op jit(solution)/shard_map/while
  1289.2 221.4 %copy-start.24 = (f32[591]{0:T(1024)S(1)}, f32[591]{0:T(1024)}, u32[]{:S(2)}) copy-start(f32[591]{0:T(1024)} %copy-done.23) | copy-start | bytes 7096 | tf_op jit(solution)/shard_map/while
  1536.5 45.1 %reduce-scatter.24.cloned.1.call-start = ((), (), s32[]{:S(2)}) async-start(), calls=%async_computation.14 | async-start | bytes 2654208 | tf_op jit(solution)/shard_map/reduce_scatter | solution.py:80
  1537.1 113.7 %reduce-scatter.22.cloned.1.call-start = ((), (), s32[]{:S(2)}) async-start(), calls=%async_computation.13 | async-start | bytes 7962624 | tf_op jit(solution)/shard_map/reduce_scatter | solution.py:79
  1537.7 192.8 %reduce-scatter.34.cloned.1.call-start = ((), (), s32[]{:S(2)}) async-start(), calls=%async_computation.19 | async-start | bytes 10616832 | tf_op jit(solution)/shard_map/reduce_scatter | solution.py:83
  1538.3 272.0 %reduce-scatter.26.cloned.1.call-start = ((), (), s32[]{:S(2)}) async-start(), calls=%async_computation.15 | async-start | bytes 10616832 | tf_op jit(solution)/shard_map/reduce_scatter | solution.py:81
  1548.1 342.1 %reduce-scatter.30.cloned.1.call-start = ((), (), s32[]{:S(2)}) async-start(), calls=%async_computation.17 | async-start | bytes 10616832 | tf_op jit(solution)/shard_map/reduce_scatter | solution.py:82
  1557.9 412.1 %reduce-scatter.38.cloned.1.call-start = ((), (), s32[]{:S(2)}) async-start(), calls=%async_computation.21 | async-start | bytes 10616832 | tf_op jit(solution)/shard_map/reduce_scatter | solution.py:84
  1567.7 439.1 %reduce-scatter.42.cloned.1.call-start = ((), (), s32[]{:S(2)}) async-start(), calls=%async_computation.23 | async-start | bytes 442368
  1568.4 403.8 %copy-start.14 = (bf16[2,591,768]{2,1,0:T(8,128)(2,1)S(1)}, bf16[2,591,768]{2,1,0:T(8,128)(2,1)}, u32[]{:S(2)}) copy-start(bf16[2,591,768]{2,1,0:T(8,128)(2,1)} %get-tuple-element.432) | copy-start | bytes 5446660
  1569.4 459.5 %reduce-scatter.46.cloned.1.call-start = ((), (), s32[]{:S(2)}) async-start(), calls=%async_computation.25 | async-start | bytes 245760
  1583.5 467.9 %reduce-scatter.44.cloned.1.call-start = ((), (), s32[]{:S(2)}) async-start(), calls=%async_computation.24 | async-start | bytes 737280
  1653.1 421.0 %reduce-scatter.36.cloned.1.call-start = ((), (), s32[]{:S(2)}) async-start(), calls=%async_computation.20 | async-start | bytes 737280 | tf_op jit(solution)/shard_map/reduce_scatter | solution.py:313
  1732.6 364.3 %reduce-scatter.28.cloned.1.call-start = ((), (), s32[]{:S(2)}) async-start(), calls=%async_computation.16 | async-start | bytes 737280 | tf_op jit(solution)/shard_map/reduce_scatter | solution.py:307
  1812.5 307.2 %reduce-scatter.32.cloned.1.call-start = ((), (), s32[]{:S(2)}) async-start(), calls=%async_computation.18 | async-start | bytes 737280 | tf_op jit(solution)/shard_map/reduce_scatter | solution.py:310
  1892.4 249.9 %reduce-scatter.40.cloned.1.call-start = ((), (), s32[]{:S(2)}) async-start(), calls=%async_computation.22 | async-start | bytes 737280 | tf_op jit(solution)/shard_map/reduce_scatter | solution.py:316
  (69 other events, 900.6 us)
Sparse Core Ops, SparseCore 0:
  28.8 74.2 all-gather.12
  104.7 70.1 all-gather.10
  488.1 264.7 all-reduce.6
  786.0 70.4 all-gather.12
  858.0 70.1 all-gather.10
  1242.3 264.8 all-reduce.6
Sparse Core Ops, SparseCore 1:
  1540.3 41.2 reduce-scatter.23
  1585.4 65.3 reduce-scatter.21
  1654.2 76.3 reduce-scatter.33
  1734.0 76.3 reduce-scatter.25
  1813.8 76.3 reduce-scatter.29
  1893.7 76.3 reduce-scatter.37
  1973.0 33.8 reduce-scatter.41
  2009.5 19.3 reduce-scatter.45
  2031.1 20.1 reduce-scatter.43
  2053.7 20.4 reduce-scatter.35
  2076.4 20.4 reduce-scatter.27
  2099.3 20.4 reduce-scatter.31
  2122.0 20.3 reduce-scatter.39
where the time goes:
time: 2160 us; the launch traced here: 2150 us
  waiting for transfers between devices  1190 us (55%)
  matrix products  454 us (21%)
  other arithmetic  302 us (14%)
  local copies, waits for them, and re-layouts  154 us (7%)
  loops' own time  25.6 us (1%)
    while x8, waiting for transfers between devices  414 us
    all_gather x2, waiting for transfers between devices, micro_step(): lax.all_gather(key_part, 'stream', axis=0, tiled=True)  128 us
    all_gather x2, waiting for transfers between devices, micro_step(): lax.all_gather(value_part, 'stream', axis=0, tiled=True)  113 us
    convert_element_type x2, other arithmetic, micro_step(): grad_scores = (probs_back * (grad_probs - inner)).astype(jnp.bfloat16)  109 us
    dot_general x2, matrix products, micro_step(): jnp.einsum('qhe,khe->hqk', grad_attended, value_heads, preferred_element_...  89 us
    add x8, other arithmetic, step_fn(): carry = jax.tree.map(jnp.add, carry, grads)  77.9 us
    reduce_scatter x1, waiting for transfers between devices, reduce_items(): lax.psum_scatter(grad_vup, 'dp', scatter_dimension=0, tiled=True)  77.6 us
    reduce_scatter x1, waiting for transfers between devices, reduce_items(): lax.psum_scatter(grad_tdown, 'dp', scatter_dimension=0, tiled=True)  77.6 us
  transfers between devices with their start and end apart: 19, of which 19 were waited for; matrix products, arithmetic and copies ran while one was open for 10% of the time, Pallas kernels for 0%

commit v1 on v0

v1 whole, which is shorter than its diff:
```python
import functools

import jax
import jax.numpy as jnp
from jax import lax
from jax.experimental import pallas as pl
from jax.experimental.pallas import tpu as pltpu
from jax.sharding import PartitionSpec as P

HEADS = 12
PATCHES = 197
OWN = 208
SLOT = 40
TILE = 256
TILES = 3
EPSILON = 1e-06
MASKED = -1e30
BF = jnp.bfloat16
F32 = jnp.float32
FULL = pl.BlockSpec(memory_space=pltpu.VMEM)
HBM = pl.BlockSpec(memory_space=pl.ANY)


def dot(left, right):
    return jnp.dot(left, right, preferred_element_type=F32)


def dot_t(left, right):
    return lax.dot_general(left, right, (((1,), (1,)), ((), ())), preferred_element_type=F32)


def t_dot(left, right):
    return lax.dot_general(left, right, (((0,), (0,)), ((), ())), preferred_element_type=F32)


def normalize(values):
    centred = values - jnp.mean(values, axis=-1, keepdims=True)
    inverse = lax.rsqrt(jnp.mean(centred * centred, axis=-1, keepdims=True) + EPSILON)
    return centred * inverse, inverse


def norm_back(grad, normed, inverse, gain):
    scaled = grad * gain
    return inverse * (
        scaled
        - jnp.mean(scaled, axis=-1, keepdims=True)
        - normed * jnp.mean(scaled * normed, axis=-1, keepdims=True)
    )


def gelu_parts(up):
    reach = jnp.abs(up) * 0.7071067811865476
    inner = 1.0 / (1.0 + 0.3275911 * reach)
    bell = jnp.exp(-0.5 * up * up)
    poly = inner * (
        0.254829592
        + inner
        * (-0.284496736 + inner * (1.421413741 + inner * (-1.453152027 + inner * 1.061405429)))
    )
    tail = 0.5 * poly * bell
    return jnp.where(up >= 0, 1.0 - tail, tail), bell * 0.3989422804014327


def attend_kernel(x_ref, ids_ref, gain_ref, shift_ref, w_ref, bias_ref, qkv_ref, out_ref, p_ref):
    width = x_ref.shape[2]
    normed, _ = normalize(x_ref[0].astype(F32))
    hidden = (normed * gain_ref[...] + shift_ref[...]).astype(BF)
    qkv = (dot(hidden, w_ref[...]) + bias_ref[...]).astype(BF)
    qkv_ref[0] = qkv
    row_ids = jnp.broadcast_to(ids_ref[0], (TILE, TILE))
    barred = jnp.where((row_ids == row_ids.T) & (row_ids >= 0), 0.0, MASKED)
    lane = lax.broadcasted_iota(jnp.int32, (1, 128), 1)
    low = (lane < 64).astype(BF)
    high = (lane >= 64).astype(BF)
    for pair in range(HEADS // 2):
        at = pair * 128
        q = qkv[:, at : at + 128] * 0.125
        k = qkv[:, width + at : width + at + 128]
        v = qkv[:, 2 * width + at : 2 * width + at + 128]
        out = None
        for side, keep in enumerate((low, high)):
            scores = dot_t(q, k * keep) + barred
            top = jnp.max(scores, axis=-1, keepdims=True)
            expo = jnp.exp(scores - top)
            total = jnp.sum(expo, axis=-1, keepdims=True)
            scale = jnp.where(top > 0.5 * MASKED, 1.0 / total, 0.0)
            probs = (expo * scale).astype(BF)
            p_ref[0, 2 * pair + side] = probs
            part = dot(probs, v * keep)
            out = part if out is None else out + part
        out_ref[0, :, at : at + 128] = out.astype(BF)


def attend(x_tiles, ids, gain, shift, w_qkv, bias):
    tiles, _, width = x_tiles.shape

    def block(*shape):
        return pl.BlockSpec((1,) + shape, lambda i: (i,) + (0,) * len(shape))

    return pl.pallas_call(
        attend_kernel,
        grid=(tiles,),
        in_specs=[block(TILE, width), block(1, TILE), FULL, FULL, FULL, FULL],
        out_specs=[block(TILE, 3 * width), block(TILE, width), block(HEADS, TILE, TILE)],
        out_shape=[
            jax.ShapeDtypeStruct((tiles, TILE, 3 * width), BF),
            jax.ShapeDtypeStruct((tiles, TILE, width), BF),
            jax.ShapeDtypeStruct((tiles, HEADS, TILE, TILE), BF),
        ],
        compiler_params=pltpu.CompilerParams(vmem_limit_bytes=56 * 2**20),
        name="attend",
    )(x_tiles, ids, gain, shift, w_qkv, bias)


def attend_back_kernel(qkv_ref, p_ref, out_ref, grad_ref, dqkv_ref):
    width = out_ref.shape[2]
    lane = lax.broadcasted_iota(jnp.int32, (1, 128), 1)
    low = lane < 64
    for pair in range(HEADS // 2):
        at = pair * 128
        q = qkv_ref[0, :, at : at + 128] * 0.125
        k = qkv_ref[0, :, width + at : width + at + 128]
        v = qkv_ref[0, :, 2 * width + at : 2 * width + at + 128].astype(F32)
        grad = grad_ref[0, :, at : at + 128]
        wide = grad.astype(F32)
        inner = pltpu.roll(wide * out_ref[0, :, at : at + 128].astype(F32), 64, 1)
        dq = dk = dv = None
        for side in range(2):
            mine = low if side == 0 else jnp.logical_not(low)
            keep = mine.astype(BF)
            left = jnp.where(mine, wide, inner).astype(BF)
            right = jnp.where(mine, v, -1.0).astype(BF)
            probs = p_ref[0, 2 * pair + side]
            dscore = (probs.astype(F32) * dot_t(left, right)).astype(BF)
            parts = dot(dscore, k * keep), t_dot(dscore, q * keep), t_dot(probs, grad * keep)
            if dq is None:
                dq, dk, dv = parts
            else:
                dq, dk, dv = dq + parts[0], dk + parts[1], dv + parts[2]
        dqkv_ref[0, :, at : at + 128] = (dq * 0.125).astype(BF)
        dqkv_ref[0, :, width + at : width + at + 128] = dk.astype(BF)
        dqkv_ref[0, :, 2 * width + at : 2 * width + at + 128] = dv.astype(BF)


def attend_back(qkv, probs, out, grad):
    tiles, _, width = out.shape

    def block(*shape):
        return pl.BlockSpec((1,) + shape, lambda i: (i,) + (0,) * len(shape))

    return pl.pallas_call(
        attend_back_kernel,
        grid=(tiles,),
        in_specs=[
            block(TILE, 3 * width),
            block(HEADS, TILE, TILE),
            block(TILE, width),
            block(TILE, width),
        ],
        out_specs=block(TILE, 3 * width),
        out_shape=jax.ShapeDtypeStruct((tiles, TILE, 3 * width), BF),
        compiler_params=pltpu.CompilerParams(vmem_limit_bytes=56 * 2**20),
        name="attend_back",
    )(qkv, probs, out, grad)


def expert_kernel(
    text_at,
    x_ref,
    att_ref,
    dy_ref,
    w_out_ref,
    gain_ref,
    shift_ref,
    bias_ref,
    up_v_ref,
    down_v_ref,
    up_t_ref,
    down_t_ref,
    out_ref,
    dmid_ref,
    datt_ref,
    dwout_ref,
    vec_ref,
    dup_ref,
    ddown_ref,
    hid_t,
    dy_t,
    acc_o,
    acc_h,
    up_w,
    down_w,
    dup_buf,
    ddown_buf,
    sems,
    out_sems,
):
    steps, _, cols = up_w.shape
    mid, hid = dmid_ref, datt_ref
    is_text = lax.axis_index("stream") == text_at

    def fetch(up_src, down_src):
        for j in range(steps):
            at = pl.ds(j * cols, cols)
            pltpu.make_async_copy(up_src.at[:, at], up_w.at[j], sems.at[0, j]).start()
            pltpu.make_async_copy(down_src.at[at, :], down_w.at[j], sems.at[1, j]).start()

    pl.when(is_text)(lambda: fetch(up_t_ref, down_t_ref))
    pl.when(jnp.logical_not(is_text))(lambda: fetch(up_v_ref, down_v_ref))

    mid[...] = x_ref[...].astype(F32) + dot(att_ref[...], w_out_ref[...])
    normed, _ = normalize(mid[...])
    hid[...] = (normed * gain_ref[...] + shift_ref[...]).astype(BF)
    hid_t[...] = hid[...].T
    dy_t[...] = dy_ref[...].T

    def stored(j, slot):
        return pltpu.make_async_copy(dup_buf.at[slot], dup_ref.at[j], out_sems.at[0, slot])

    def stored_down(j, slot):
        return pltpu.make_async_copy(ddown_buf.at[slot], ddown_ref.at[j], out_sems.at[1, slot])

    @pl.loop(0, steps)
    def _(j):
        at = pl.ds(j * cols, cols)
        pltpu.make_async_copy(up_v_ref.at[:, at], up_w.at[j], sems.at[0, j]).wait()
        pltpu.make_async_copy(down_v_ref.at[at, :], down_w.at[j], sems.at[1, j]).wait()
        up = dot(hid[...], up_w[j])
        grad = dot_t(dy_ref[...], down_w[j])
        cdf, pdf = gelu_parts(up)
        activ = (up * cdf).astype(BF)
        grad_up = (grad * (cdf + up * pdf)).astype(BF)
        part_o = dot(activ, down_w[j])
        part_h = dot_t(grad_up, up_w[j])

        @pl.when(j == 0)
        def _():
            acc_o[...] = part_o
            acc_h[...] = part_h

        @pl.when(j > 0)
        def _():
            acc_o[...] += part_o
            acc_h[...] += part_h

        slot = lax.rem(j, 2)

        @pl.when(j > 1)
        def _():
            stored(j - 2, slot).wait()
            stored_down(j - 2, slot).wait()

        dup_buf[slot] = dot(hid_t[...], grad_up).astype(BF)
        stored(j, slot).start()
        ddown_buf[slot] = dot(dy_t[...], activ).astype(BF)
        stored_down(j, slot).start()

    out_ref[...] = (mid[...] + acc_o[...] + bias_ref[...]).astype(BF)
    normed, inverse = normalize(mid[...])
    grad = acc_h[...]
    wide = dy_ref[...].astype(F32)
    vec_ref[0:1, :] = jnp.sum(grad * normed, axis=0, keepdims=True)
    vec_ref[1:2, :] = jnp.sum(grad, axis=0, keepdims=True)
    vec_ref[2:3, :] = jnp.sum(wide, axis=0, keepdims=True)
    grad_mid = wide + norm_back(grad, normed, inverse, gain_ref[...])
    dmid_ref[...] = grad_mid
    branch = grad_mid.astype(BF)
    datt_ref[...] = dot_t(branch, w_out_ref[...]).astype(BF)
    dwout_ref[...] = t_dot(att_ref[...], branch).astype(BF)
    for j in range(steps - 2, steps):
        stored(j, j % 2).wait()
        stored_down(j, j % 2).wait()


def expert(x, att, dy, w_out, gain, shift, bias, vis_up, vis_down, txt_up, txt_down):
    rows, width = x.shape
    ff = vis_up.shape[1]
    steps = 3
    cols = ff // steps
    return pl.pallas_call(
        functools.partial(expert_kernel, 3),
        in_specs=[FULL] * 7 + [HBM] * 4,
        out_specs=[FULL] * 5 + [HBM] * 2,
        out_shape=[
            jax.ShapeDtypeStruct((rows, width), BF),
            jax.ShapeDtypeStruct((rows, width), F32),
            jax.ShapeDtypeStruct((rows, width), BF),
            jax.ShapeDtypeStruct((width, width), BF),
            jax.ShapeDtypeStruct((8, width), F32),
            jax.ShapeDtypeStruct((steps, width, cols), BF),
            jax.ShapeDtypeStruct((steps, width, cols), BF),
        ],
        scratch_shapes=[
            pltpu.VMEM((width, rows), BF),
            pltpu.VMEM((width, rows), BF),
            pltpu.VMEM((rows, width), F32),
            pltpu.VMEM((rows, width), F32),
            pltpu.VMEM((steps, width, cols), BF),
            pltpu.VMEM((steps, cols, width), BF),
            pltpu.VMEM((2, width, cols), BF),
            pltpu.VMEM((2, width, cols), BF),
            pltpu.SemaphoreType.DMA((2, steps)),
            pltpu.SemaphoreType.DMA((2, 2)),
        ],
        compiler_params=pltpu.CompilerParams(vmem_limit_bytes=63 * 2**20),
        name="expert",
    )(x, att, dy, w_out, gain, shift, bias, vis_up, vis_down, txt_up, txt_down)


def project_back_kernel(x_ref, dqkv_ref, gain_ref, shift_ref, w_ref, dx_ref, dw_ref, vec_ref, acc):
    i = pl.program_id(0)
    gain = gain_ref[...]
    normed, inverse = normalize(x_ref[0].astype(F32))
    hidden = (normed * gain + shift_ref[...]).astype(BF)
    dqkv = dqkv_ref[0]
    grad = dot_t(dqkv, w_ref[...])
    dx_ref[0] = norm_back(grad, normed, inverse, gain).astype(BF)
    width = x_ref.shape[2]
    part = t_dot(hidden, dqkv)
    ones = jnp.ones((8, TILE), BF)
    sums = dot(ones, dqkv)[0:1]
    vec = jnp.concatenate(
        [
            jnp.sum(grad * normed, axis=0, keepdims=True),
            jnp.sum(grad, axis=0, keepdims=True),
            sums[:, :width],
            sums[:, 2 * width :],
        ],
        axis=0,
    )

    @pl.when(i == 0)
    def _():
        acc[...] = part
        vec_ref[0:4, :] = vec

    @pl.when(i > 0)
    def _():
        acc[...] += part
        vec_ref[0:4, :] += vec

    @pl.when(i == pl.num_programs(0) - 1)
    def _():
        dw_ref[...] = acc[...].astype(BF)


def project_back(x_tiles, dqkv, gain, shift, w_qkv):
    tiles, _, width = x_tiles.shape

    def block(*shape):
        return pl.BlockSpec((1,) + shape, lambda i: (i,) + (0,) * len(shape))

    return pl.pallas_call(
        project_back_kernel,
        grid=(tiles,),
        in_specs=[block(TILE, width), block(TILE, 3 * width), FULL, FULL, FULL],
        out_specs=[block(TILE, width), FULL, FULL],
        out_shape=[
            jax.ShapeDtypeStruct((tiles, TILE, width), BF),
            jax.ShapeDtypeStruct((width, 3 * width), BF),
            jax.ShapeDtypeStruct((8, width), F32),
        ],
        scratch_shapes=[pltpu.VMEM((width, 3 * width), F32)],
        compiler_params=pltpu.CompilerParams(vmem_limit_bytes=56 * 2**20),
        name="project_back",
    )(x_tiles, dqkv, gain, shift, w_qkv)


def pad_rows(block):
    micro, rows, width = block.shape
    thirds = block.reshape(micro, TILES, PATCHES, width)
    thirds = jnp.pad(thirds, ((0, 0), (0, 0), (0, OWN - PATCHES), (0, 0)))
    return thirds.reshape(micro, TILES * OWN, width)


def unpad_rows(block):
    micro, _, width = block.shape
    thirds = block.reshape(micro, TILES, OWN, width)[:, :, :PATCHES]
    return thirds.reshape(micro, TILES * PATCHES, width)


def plan(lengths, pairs, is_text, own_stream):
    micro, items = lengths.shape
    finish = jnp.cumsum(lengths, axis=1)
    starts = finish - lengths
    numbers = jnp.arange(items, dtype=jnp.int32)
    match = pairs[:, :, None] == numbers
    start = jnp.sum(jnp.where(match, starts[:, None, :], 0), axis=2).reshape(micro, 3, TILES)
    length = jnp.sum(jnp.where(match, lengths[:, None, :], 0), axis=2).reshape(micro, 3, TILES)
    paired = (pairs >= 0).reshape(micro, 3, TILES)
    rank = jnp.where(paired, jnp.cumsum(paired.astype(jnp.int32), axis=2) - 1, -1)
    takes = rank[:, :, :, None] == jnp.arange(2)
    slot_start = jnp.sum(jnp.where(takes, start[..., None], 0), axis=2)
    slot_length = jnp.sum(jnp.where(takes, length[..., None], 0), axis=2)
    step = jnp.arange(SLOT, dtype=jnp.int32)
    slot_rows = jnp.where(step < slot_length[..., None], slot_start[..., None] + step, -1)
    next_rows = jnp.broadcast_to(
        PATCHES * jnp.arange(1, TILES, dtype=jnp.int32)[:, None] + step, (micro, TILES - 1, SLOT)
    )
    wanted = jnp.concatenate([slot_rows.reshape(micro, -1), next_rows.reshape(micro, -1)], axis=1)
    place = jnp.arange(TILES * OWN, dtype=jnp.int32)
    row_at = jnp.where(place % OWN < PATCHES, place // OWN * PATCHES + place % OWN, -2)
    picks = (wanted[:, :, None] == row_at).astype(BF)
    item_paired = jnp.any(match, axis=1)
    rows = jnp.arange(TILES * PATCHES + SLOT, dtype=jnp.int32)
    member = (rows[:, None] >= starts[:, None, :]) & (rows[:, None] < finish[:, None, :])
    code = jnp.where(item_paired, -1, numbers + items * (starts // PATCHES))
    row_code = jnp.sum(jnp.where(member, code[:, None, :] + 1, 0), axis=2) - 1
    tile = jnp.arange(TILES, dtype=jnp.int32)[:, None]
    own_code = row_code[:, : TILES * PATCHES].reshape(micro, TILES, PATCHES)
    next_code = jnp.stack(
        [row_code[:, PATCHES * (t + 1) : PATCHES * (t + 1) + SLOT] for t in range(TILES)], axis=1
    )

    def here(codes):
        return jnp.where((codes >= 0) & (codes // items == tile), codes, -1)

    def lay(own, extra):
        gap = jnp.full((micro, TILES, OWN - PATCHES), -1, jnp.int32)
        end = jnp.full((micro, TILES, TILE - OWN - SLOT), -1, jnp.int32)
        return jnp.concatenate([own, gap, extra, end], axis=2)

    text_ids = lay(here(own_code), here(next_code))
    own_length = lax.dynamic_index_in_dim(length, jnp.minimum(own_stream, 2), 1, keepdims=False)
    own_takes = lax.dynamic_index_in_dim(takes, jnp.minimum(own_stream, 2), 1, keepdims=False)
    image_ids = lay(
        jnp.zeros((micro, TILES, PATCHES), jnp.int32),
        jnp.where(step < own_length[..., None], 0, -1),
    )
    ids = jnp.where(is_text, text_ids, image_ids)
    return picks, own_takes.astype(BF), ids.reshape(micro * TILES, 1, TILE)


def spread(padded, picks, own_takes, is_text):
    micro, _, width = padded.shape
    picked = lax.dot_general(
        picks, padded, (((2,), (1,)), ((0,), (0,))), preferred_element_type=F32
    ).astype(BF)
    near = picked[:, 6 * SLOT :].reshape(micro, TILES - 1, SLOT, width)
    near = jnp.concatenate([near, jnp.zeros((micro, 1, SLOT, width), BF)], axis=1)
    sent = picked[:, : 6 * SLOT].reshape(micro, 3, 2 * SLOT, width)
    far = sum(lax.ppermute(sent[:, s], "stream", [(3, s)]) for s in range(3))
    far = far.reshape(micro, 1, 2, SLOT, width) * own_takes[:, :, :, None, None]
    return jnp.where(is_text, near, far[:, :, 0] + far[:, :, 1])


def collect(extra, picks, own_takes, is_text):
    micro, _, _, width = extra.shape
    mine = extra[:, :, None] * own_takes[:, :, :, None, None]
    mine = (mine[:, 0] + mine[:, 1] + mine[:, 2]).reshape(micro, 2 * SLOT, width)
    parts = [lax.ppermute(mine, "stream", [(s, 3)]) for s in range(3)]
    parts.append(extra[:, : TILES - 1].reshape(micro, (TILES - 1) * SLOT, width))
    rows = jnp.concatenate(parts, axis=1)
    scale = jnp.where(is_text, 1.0, 0.0).astype(BF)
    return lax.dot_general(
        picks * scale, rows, (((1,), (1,)), ((0,), (0,))), preferred_element_type=F32
    ).astype(BF)


def reduce_all(vectors, dw_qkv, dw_out, dup, ddown):
    width = dw_qkv.shape[0]
    shard = width // lax.axis_size("dp")
    vectors = lax.psum(vectors, ("dp", "stream"))
    vectors = lax.dynamic_slice_in_dim(vectors, lax.axis_index("dp") * shard, shard, axis=1)

    def over_items(grad, dim):
        return lax.psum_scatter(grad, "dp", scatter_dimension=dim, tiled=True)

    def over_blocks(grad):
        return lax.psum_scatter(grad, "stream", scatter_dimension=1, tiled=True).astype(F32)

    dup = over_items(dup, 0)
    ddown = over_items(ddown, 1)
    qkv = over_blocks(over_items(dw_qkv, 0))
    out = over_blocks(over_items(dw_out, 0))
    up = dup.reshape(dup.shape[0], 4, -1).transpose(1, 0, 2)
    down = ddown.reshape(4, -1, ddown.shape[1])
    up = lax.all_to_all(up, "stream", 0, 0).astype(F32)
    down = lax.all_to_all(down, "stream", 0, 0).astype(F32)
    return (
        vectors,
        qkv,
        out,
        up[0] + up[1] + up[2],
        (down[0] + down[1] + down[2]).T,
        up[3],
        down[3].T,
    )


def shards(
    tokens,
    text_lengths,
    pair_text,
    ln1_gain,
    ln1_bias,
    w_qkv,
    q_bias,
    v_bias,
    w_out,
    ln2_gain,
    ln2_bias,
    vis_up,
    vis_down,
    vis_bias,
    txt_up,
    txt_down,
    txt_bias,
    cotangent,
):
    micro = tokens.shape[0]
    width = tokens.shape[4]
    own_stream = lax.axis_index("stream")
    is_text = own_stream == 3
    gain1, shift1, gain2, shift2 = (
        v.astype(F32)[None] for v in (ln1_gain, ln1_bias, ln2_gain, ln2_bias)
    )
    bias = jnp.where(is_text, txt_bias, vis_bias).astype(F32)[None]
    qkv_bias = jnp.concatenate([q_bias, jnp.zeros_like(q_bias), v_bias]).astype(F32)[None]
    picks, own_takes, ids = plan(text_lengths[:, 0], pair_text[:, 0], is_text, own_stream)

    def tiled(own, extra):
        own = own.reshape(micro, TILES, OWN, width)
        extra = jnp.pad(extra, ((0, 0), (0, 0), (0, TILE - OWN - SLOT), (0, 0)))
        return jnp.concatenate([own, extra], axis=2).reshape(micro * TILES, TILE, width)

    def parted(tiles):
        tiles = tiles.reshape(micro, TILES, TILE, width)
        return tiles[:, :, :OWN].reshape(micro, TILES * OWN, width), tiles[:, :, OWN : OWN + SLOT]

    x = pad_rows(tokens[:, 0, 0])
    dy = pad_rows(cotangent[:, 0, 0])
    x_tiles = tiled(x, spread(x, picks, own_takes, is_text))
    qkv, att_tiles, probs = attend(x_tiles, ids, gain1, shift1, w_qkv, qkv_bias)
    att_own, att_extra = parted(att_tiles)
    att = att_own + collect(att_extra, picks, own_takes, is_text)
    flat = (micro * TILES * OWN, width)
    out, dmid, datt, dw_out, vec2, dup, ddown = expert(
        x.reshape(flat),
        att.reshape(flat),
        dy.reshape(flat),
        w_out,
        gain2,
        shift2,
        bias,
        vis_up,
        vis_down,
        txt_up,
        txt_down,
    )
    datt = datt.reshape(micro, TILES * OWN, width)
    datt_tiles = tiled(datt, spread(datt, picks, own_takes, is_text))
    dqkv = attend_back(qkv, probs, att_tiles, datt_tiles)
    dx_tiles, dw_qkv, vec1 = project_back(x_tiles, dqkv, gain1, shift1, w_qkv)
    dx_own, dx_extra = parted(dx_tiles)
    dx = (
        dmid.reshape(micro, TILES * OWN, width)
        + dx_own.astype(F32)
        + collect(dx_extra, picks, own_takes, is_text).astype(F32)
    )
    text_scale = jnp.where(is_text, 1.0, 0.0)
    vectors = jnp.concatenate(
        [vec1[0:4], vec2[0:2], vec2[2:3] * (1.0 - text_scale), vec2[2:3] * text_scale], axis=0
    )
    dup = jnp.concatenate(list(dup), axis=1)
    ddown = jnp.concatenate(list(ddown), axis=1)
    vectors, g_qkv, g_out, g_vup, g_vdown, g_tup, g_tdown = reduce_all(
        vectors, dw_qkv, dw_out, dup, ddown
    )
    return (
        unpad_rows(out.reshape(micro, TILES * OWN, width)).reshape(tokens.shape),
        unpad_rows(dx).astype(BF).reshape(tokens.shape),
        vectors[0],
        vectors[1],
        g_qkv,
        vectors[2],
        vectors[3],
        g_out,
        vectors[4],
        vectors[5],
        g_vup,
        g_vdown,
        vectors[6],
        g_tup,
        g_tdown,
        vectors[7],
    )


def solution(mesh):
    rows = P(None, "dp", "stream", None, None)
    lists = P(None, "dp", None)
    vector, matrix = P("dp"), P("dp", "stream")
    in_specs = (rows, lists, lists) + (P(),) * 14 + (rows,)
    out_specs = (
        rows,
        rows,
        vector,
        vector,
        matrix,
        vector,
        vector,
        matrix,
        vector,
        vector,
        matrix,
        matrix,
        vector,
        matrix,
        matrix,
        vector,
    )
    return jax.shard_map(shards, mesh=mesh, in_specs=in_specs, out_specs=out_specs, check_vma=False)
```

time: 2160 us -> 436 us (0.20)
  waiting for transfers between devices: 1190 us -> 135 us
  matrix products: 454 us -> 10 us
  other arithmetic: 302 us -> 21.3 us
  Pallas kernels: 0 us -> 131 us
  local copies, waits for them, and re-layouts: 154 us -> 43.5 us
  starting transfers between devices: 1.55 us -> 33.7 us
  blocking collectives: 11.7 us -> 39.8 us
  loops' own time: 25.6 us -> 0 us
    dot_general x36 -> x4, matrix products: 454 us -> 10 us  [the longest x2 6.58 us: collect(): lax.dot_general(picks * scale, rows, (((1,), (1,)), ((0,), (0,))), prefer...]
    while x8 -> x0, waiting for transfers between devices: 414 us -> none
    reduce_scatter x10 -> x3, waiting for transfers between devices: 474 us -> 68 us  [over_items(): return lax.psum_scatter(grad, 'dp', scatter_dimension=dim, tiled=True)]
    all_gather x4 -> x0, waiting for transfers between devices: 240 us -> none  [the longest x2 128 us: micro_step(): lax.all_gather(key_part, 'stream', axis=0, tiled=True)]
    convert_element_type x26 -> x7, other arithmetic: 136 us -> 2.16 us  [the longest x2 1.36 us: over_blocks(): lax.psum_scatter(grad, 'stream', scatter_dimension=1, tiled=True)]
    pallas_call x0 -> x4, Pallas kernels: none -> 131 us  [the longest x1 59.8 us: expert(): pl.pallas_call(functools.partial(expert_kernel, 3), in_specs=[FULL] * 7 +...]
    add x12 -> x5, other arithmetic: 87.8 us -> 1.41 us  [the longest x2 1.27 us: spread(): far = sum((lax.ppermute(sent[:, s], 'stream', [(3, s)]) for s in range(3)))]
    reduce_sum x18 -> x3, other arithmetic: 61.1 us -> 1.3 us  [the longest x1 0.91 us: plan(): jnp.sum(jnp.where(match, starts[:, None, :], 0), axis=2)]
  transfers between devices with their start and end apart: 19 -> 20, of which waited for: 19 -> 7; matrix products, arithmetic and copies ran while one was open for 10% -> 10% of each run, Pallas kernels for 0% -> 10%
where the time goes in v1:
time: 436 us; the launch traced here: 429 us
  waiting for transfers between devices  135 us (31%)
  Pallas kernels  131 us (30%)
  local copies, waits for them, and re-layouts  43.5 us (10%)
  blocking collectives  39.8 us (9%)
  starting transfers between devices  33.7 us (8%)
  other arithmetic  21.3 us (5%)
  between operations  15 us (3%)
  matrix products  10 us (2%)
    reduce_scatter x3, waiting for transfers between devices, over_items(): return lax.psum_scatter(grad, 'dp', scatter_dimension=dim, tiled=True)  68 us
    pallas_call x1, Pallas kernels, expert(): pl.pallas_call(functools.partial(expert_kernel, 3), in_specs=[FULL] * 7 +...  59.8 us
    psum x1, blocking collectives, reduce_all(): vectors = lax.psum(vectors, ('dp', 'stream'))  39.8 us
    unnamed x9, waiting for transfers between devices  34.2 us
    ppermute x6, waiting for transfers between devices, spread(): far = sum((lax.ppermute(sent[:, s], 'stream', [(3, s)]) for s in range(3)))  33.1 us
    pallas_call x1, Pallas kernels, attend(): pl.pallas_call(attend_kernel, grid=(tiles,), in_specs=[block(TILE, width)...  27.8 us
    pallas_call x1, Pallas kernels, project_back(): pl.pallas_call(project_back_kernel, grid=(tiles,), in_specs=[block(TILE,...  22.3 us
    pallas_call x1, Pallas kernels, attend_back(): pl.pallas_call(attend_back_kernel, grid=(tiles,), in_specs=[block(TILE, 3...  20.7 us
  transfers between devices with their start and end apart: 20, of which 7 were waited for; matrix products, arithmetic and copies ran while one was open for 10% of the time, Pallas kernels for 10%

profile of v1, /device:TPU:0, one launch (start us, length us, event | category | flops | bytes accessed | tf_op | source)
XLA Modules:
  0.0 429.2 jit_solution(9760558462657134157)
XLA Ops:
  24.0 12.2 %collective-permute-done = bf16[2,80,768]{2,1,0:T(8,128)(2,1)} collective-permute-done((bf16[2,80,768]{2,1,0:T(8,128)(2,1)S(1)}, bf16[2,80,768]{2,1,0:T(8,128)(2,1)}, u32[]{:S(2)}, u32[]{:S(2)}) %collective-permute-start) | collective-permute-done | bytes 245792 | tf_op jit(solution)/shard_map/ppermute | solution.py:442
  39.2 27.8 %attend.1 = (bf16[6,256,2304]{2,1,0:T(8,128)(2,1)}, bf16[6,256,768]{2,1,0:T(8,128)(2,1)}, bf16[6,12,256,256]{3,2,1,0:T(8,128)(2,1)}) custom-call(bf16[6,256,768]{2,1,0:T(8,128)(2,1)} %bitcast.146, s32[6,1,256]{2,1,0:T(1,128)} %broadcast_select_fusion.ids_ref, f32[1,768]{1,0:T(1,128)} %reshape.385.gain_ref, f32[1,768]{1,0:T(1,128)} %reshape.386.shift_ref, ...), custom_call_target="tpu_custom_call" | custom-call | tf_op jit(solution)/shard_map/attend/pallas_call | solution.py:100
  69.7 6.9 %collective-permute-start.3 = (bf16[2,80,768]{2,1,0:T(8,128)(2,1)S(1)}, bf16[2,80,768]{2,1,0:T(8,128)(2,1)S(1)}, u32[]{:S(2)}, u32[]{:S(2)}) collective-permute-start(bf16[2,80,768]{2,1,0:T(8,128)(2,1)S(1)} %bitcast.184), channel_id=1, source_target_pairs={{0,3},{4,7},{8,11},{12,15},{16,19},{20,23},{24,27},{28,31}} | collective-permute-start | bytes 737288 | tf_op jit(solution)/shard_map/ppermute | solution.py:451
  81.2 2.6 bitcast_add_fusion
  83.8 59.8 %expert.1 = (bf16[1248,768]{1,0:T(8,128)(2,1)}, f32[1248,768]{1,0:T(8,128)}, bf16[1248,768]{1,0:T(8,128)(2,1)}, bf16[768,768]{1,0:T(8,128)(2,1)}, f32[8,768]{1,0...) custom-call(bf16[1248,768]{1,0:T(8,128)(2,1)} %bitcast.150, bf16[1248,768]{1,0:T(8,128)(2,1)} %bitcast.163, ...), custom_call_target="tpu_custom_call" | custom-call | tf_op jit(solution)/shard_map/expert/pallas_call | solution.py:280
  143.7 5.2 %slice_bitcast_fusion.2 = (bf16[768,1024]{1,0:T(8,128)(2,1)S(1)}, bf16[768,1024]{1,0:T(8,128)(2,1)S(1)}, bf16[768,1024]{1,0:T(8,128)(2,1)S(1)}, bf16[768,1024]{1...) fusion(bf16[3,768,1024]{2,1,0:T(8,128)(2,1)} %get-tuple-element.41, ...), kind=kLoop, calls=%fused_computation.17 | loop fusion | bytes 18874368 | tf_op jit(solution)/shard_map/unstack | solution.py:566
  151.1 6.7 %copy.126 = bf16[768,3072]{0,1:T(8,128)(2,1)} copy(bf16[768,3072]{1,0:T(8,128)(2,1)} %pad_maximum_fusion.1) | data formatting | bytes 9437184
  158.7 2.5 fusion.11
  164.0 20.9 %collective-permute-done.6 = bf16[2,80,768]{2,1,0:T(8,128)(2,1)S(1)} collective-permute-done((bf16[2,80,768]{2,1,0:T(8,128)(2,1)S(1)}, bf16[2,80,768]{2,1,0:T(8,128)(2,1)S(1)}, u32[]{:S(2)}, u32[]{:S(2)}) %collective-permute-start.6) | collective-permute-done | bytes 245792 | tf_op jit(solution)/shard_map/ppermute | solution.py:442
  186.8 20.7 %attend_back.1.dqkv_ref = bf16[6,256,2304]{2,1,0:T(8,128)(2,1)} custom-call(bf16[6,256,2304]{2,1,0:T(8,128)(2,1)} %get-tuple-element.32.qkv_ref, bf16[6,12,256,256]{3,2,1,0:T(8,128)(2,1)} %get-tuple-element.33.p_ref, bf16[6,256,768]{2,1,0:T(8,128)(2,1)} %get-tuple-element.29.out_ref, bf16[6,256,768]{2,1,0:T(8,128)(2,1)} %pad_maximum_fusion.2.grad_ref), custom_call_target="tpu_custom_call" | custom-call | tf_op jit(solution)/shard_map/attend_back/pallas_call | solution.py:151
  207.4 22.3 %project_back.1 = (bf16[6,256,768]{2,1,0:T(8,128)(2,1)}, bf16[768,2304]{1,0:T(8,128)(2,1)}, f32[8,768]{1,0:T(8,128)}) custom-call(bf16[6,256,768]{2,1,0:T(8,128)(2,1)} %bitcast.147, bf16[6,256,2304]{2,1,0:T(8,128)(2,1)} %attend_back.1.dqkv_ref, f32[1,768]{1,0:T(1,128)} %reshape.385.gain_ref, f32[1,768]{1,0:T(1,128)} %reshape.386.shift_ref, ...), custom_call_target="tpu_custom_call" | custom-call | tf_op jit(solution)/shard_map/project_back/pallas_call | solution.py:353
  229.8 3.5 pad_maximum_fusion
  235.0 2.6 copy.115
  240.7 5.3 %all-to-all-start.1 = ((bf16[4,192,384]{2,1,0:T(8,128)(2,1)}), bf16[4,192,384]{2,1,0:T(8,128)(2,1)S(1)}, u32[]{:S(2)}, u32[]{:S(2)}) async-start(bf16[4,192,384]{2,1,0:T(8,128)(2,1)} %bitcast.63), calls=%async_computation.4 | async-start | bytes 1179648 | tf_op jit(solution)/shard_map/all_to_all | solution.py:479
  246.8 13.4 %reduce-scatter.15.cloned.1.call-done = bf16[96,768]{1,0:T(8,128)(2,1)} async-done(((bf16[768,768]{1,0:T(8,128)(2,1)}), bf16[96,768]{1,0:T(8,128)(2,1)}) %reduce-scatter.15.cloned.1.call-update) | async-done | bytes 147472 | tf_op jit(solution)/shard_map/reduce_scatter | solution.py:467
  264.9 5.8 %collective-permute-start.9 = (bf16[2,80,768]{2,1,0:T(8,128)(2,1)S(1)}, bf16[2,80,768]{2,1,0:T(8,128)(2,1)}, u32[]{:S(2)}, u32[]{:S(2)}) collective-permute-start(bf16[2,80,768]{2,1,0:T(8,128)(2,1)S(1)} %bitcast.180), channel_id=1, source_target_pairs={{0,3},{4,7},{8,11},{12,15},{16,19},{20,23},{24,27},{28,31}} | collective-permute-start | bytes 737288 | tf_op jit(solution)/shard_map/ppermute | solution.py:451
  270.7 41.1 %reduce-scatter.13.cloned.1.call-done = bf16[96,2304]{1,0:T(8,128)(2,1)} async-done(((bf16[768,2304]{1,0:T(8,128)(2,1)}), bf16[96,2304]{1,0:T(8,128)(2,1)}) %reduce-scatter.13.cloned.1.call-update) | async-done | bytes 442384 | tf_op jit(solution)/shard_map/reduce_scatter | solution.py:467
  313.9 39.8 %psum.7 = f32[8,768]{1,0:T(8,128)S(1)} all-reduce(f32[8,768]{1,0:T(8,128)S(1)} %pad_maximum_fusion.3), channel_id=1, replica_groups=mesh['dp'=8,'stream'=4] {'dp','stream'}, use_global_device_ids=true, to_apply=%region_8.9 | all-reduce | flops 6144 | bytes 49152 | tf_op jit(solution)/shard_map/psum | solution.py:463
  355.9 13.6 %reduce-scatter.17.cloned.1.call-done = bf16[96,3072]{1,0:T(8,128)(2,1)} async-done(((bf16[768,3072]{1,0:T(8,128)(2,1)}), bf16[96,3072]{1,0:T(8,128)(2,1)}) %reduce-scatter.17.cloned.1.call-update) | async-done | bytes 589840 | tf_op jit(solution)/shard_map/reduce_scatter | solution.py:467
  371.4 4.8 %all-to-all-start = ((bf16[4,96,768]{2,1,0:T(8,128)(2,1)}), bf16[4,96,768]{2,1,0:T(8,128)(2,1)S(1)}, u32[]{:S(2)}, u32[]{:S(2)}) async-start(bf16[4,96,768]{2,1,0:T(8,128)(2,1)} %bitcast.144), calls=%async_computation.3 | async-start | bytes 1179648 | tf_op jit(solution)/shard_map/all_to_all | solution.py:478
  376.8 3.9 fusion.2
  380.9 2.6 copy.120
  383.5 9.0 %reduce-scatter.21.cloned.1.call-done = bf16[192,96]{1,0:T(8,128)(2,1)} async-done(((bf16[768,96]{1,0:T(8,128)(2,1)}), bf16[192,96]{1,0:T(8,128)(2,1)}) %reduce-scatter.21.cloned.1.call-update) | async-done | bytes 36880
  394.1 24.4 %reduce-scatter.19.cloned.1.call-done = bf16[576,96]{1,0:T(8,128)(2,1)} async-done(((bf16[2304,96]{1,0:T(8,128)(2,1)}), bf16[576,96]{1,0:T(8,128)(2,1)}) %reduce-scatter.19.cloned.1.call-update) | async-done | bytes 110608
  (187 shorter events, 56.8 us)
Async XLA Ops:
  7.2 231.4 %reduce-scatter.23.cloned.1.call-start = ((), (), s32[]{:S(2)}) async-start(), calls=%async_computation.13 | async-start | bytes 5308416
  14.7 23.0 %copy-start = (bf16[2,3,208,768]{3,2,1,0:T(8,128)(2,1)}, bf16[2,3,208,768]{3,2,1,0:T(8,128)(2,1)S(1)}, u32[]{:S(2)}) copy-start(bf16[2,3,208,768]{3,2,1,0:T(8,128)(2,1)S(1)} %pad.16) | copy-start | bytes 5750788
  16.5 7.5 %collective-permute-start.1 = (bf16[2,80,768]{2,1,0:T(8,128)(2,1)}, bf16[2,80,768]{2,1,0:T(8,128)(2,1)}, u32[]{:S(2)}, u32[]{:S(2)}) collective-permute-start(bf16[2,80,768]{2,1,0:T(8,128)(2,1)} %get-tuple-element.59), channel_id=1, source_target_pairs={{3,1},{7,5},{11,9},{15,13},{19,17},{23,21},{27,25},{31,29}} | collective-permute-start | bytes 737288 | tf_op jit(solution)/shard_map/ppermute | solution.py:442
  17.9 18.3 %collective-permute-start = (bf16[2,80,768]{2,1,0:T(8,128)(2,1)S(1)}, bf16[2,80,768]{2,1,0:T(8,128)(2,1)}, u32[]{:S(2)}, u32[]{:S(2)}) collective-permute-start(bf16[2,80,768]{2,1,0:T(8,128)(2,1)S(1)} %get-tuple-element.60), channel_id=1, source_target_pairs={{3,0},{7,4},{11,8},{15,12},{19,16},{23,20},{27,24},{31,28}} | collective-permute-start | bytes 737288 | tf_op jit(solution)/shard_map/ppermute | solution.py:442
  19.2 17.0 %collective-permute-start.2 = (bf16[2,80,768]{2,1,0:T(8,128)(2,1)S(1)}, bf16[2,80,768]{2,1,0:T(8,128)(2,1)}, u32[]{:S(2)}, u32[]{:S(2)}) collective-permute-start(bf16[2,80,768]{2,1,0:T(8,128)(2,1)S(1)} %get-tuple-element.61), channel_id=1, source_target_pairs={{3,2},{7,6},{11,10},{15,14},{19,18},{23,22},{27,26},{31,30}} | collective-permute-start | bytes 737288 | tf_op jit(solution)/shard_map/ppermute | solution.py:442
  68.4 12.8 %collective-permute-start.5 = (bf16[2,80,768]{2,1,0:T(8,128)(2,1)S(1)}, bf16[2,80,768]{2,1,0:T(8,128)(2,1)S(1)}, u32[]{:S(2)}, u32[]{:S(2)}) collective-permute-start(bf16[2,80,768]{2,1,0:T(8,128)(2,1)S(1)} %bitcast.182), channel_id=1, source_target_pairs={{2,3},{6,7},{10,11},{14,15},{18,19},{22,23},{26,27},{30,31}} | collective-permute-start | bytes 737288 | tf_op jit(solution)/shard_map/ppermute | solution.py:451
  69.0 12.1 %collective-permute-start.4 = (bf16[2,80,768]{2,1,0:T(8,128)(2,1)S(1)}, bf16[2,80,768]{2,1,0:T(8,128)(2,1)S(1)}, u32[]{:S(2)}, u32[]{:S(2)}) collective-permute-start(bf16[2,80,768]{2,1,0:T(8,128)(2,1)S(1)} %bitcast.183), channel_id=1, source_target_pairs={{1,3},{5,7},{9,11},{13,15},{17,19},{21,23},{25,27},{29,31}} | collective-permute-start | bytes 737288 | tf_op jit(solution)/shard_map/ppermute | solution.py:451
  69.7 11.5 %collective-permute-start.3 = (bf16[2,80,768]{2,1,0:T(8,128)(2,1)S(1)}, bf16[2,80,768]{2,1,0:T(8,128)(2,1)S(1)}, u32[]{:S(2)}, u32[]{:S(2)}) collective-permute-start(bf16[2,80,768]{2,1,0:T(8,128)(2,1)S(1)} %bitcast.184), channel_id=1, source_target_pairs={{0,3},{4,7},{8,11},{12,15},{16,19},{20,23},{24,27},{28,31}} | collective-permute-start | bytes 737288 | tf_op jit(solution)/shard_map/ppermute | solution.py:451
  157.9 102.2 %reduce-scatter.15.cloned.1.call-start = ((), (), s32[]{:S(2)}) async-start(), calls=%async_computation.9 | async-start | bytes 1327104 | tf_op jit(solution)/shard_map/reduce_scatter | solution.py:467
  158.6 153.1 %reduce-scatter.13.cloned.1.call-start = ((), (), s32[]{:S(2)}) async-start(), calls=%async_computation.8 | async-start | bytes 3981312 | tf_op jit(solution)/shard_map/reduce_scatter | solution.py:467
  161.3 2.7 collective-permute-start.7
  162.0 22.9 %collective-permute-start.6 = (bf16[2,80,768]{2,1,0:T(8,128)(2,1)S(1)}, bf16[2,80,768]{2,1,0:T(8,128)(2,1)S(1)}, u32[]{:S(2)}, u32[]{:S(2)}) collective-permute-start(bf16[2,80,768]{2,1,0:T(8,128)(2,1)S(1)} %get-tuple-element.57), channel_id=1, source_target_pairs={{3,0},{7,4},{11,8},{15,12},{19,16},{23,20},{27,24},{31,28}} | collective-permute-start | bytes 737288 | tf_op jit(solution)/shard_map/ppermute | solution.py:442
  163.3 21.6 %collective-permute-start.8 = (bf16[2,80,768]{2,1,0:T(8,128)(2,1)S(1)}, bf16[2,80,768]{2,1,0:T(8,128)(2,1)S(1)}, u32[]{:S(2)}, u32[]{:S(2)}) collective-permute-start(bf16[2,80,768]{2,1,0:T(8,128)(2,1)S(1)} %get-tuple-element.58), channel_id=1, source_target_pairs={{3,2},{7,6},{11,10},{15,14},{19,18},{23,22},{27,26},{31,30}} | collective-permute-start | bytes 737288 | tf_op jit(solution)/shard_map/ppermute | solution.py:442
  164.0 21.2 %copy-start.3 = (bf16[1248,768]{1,0:T(8,128)(2,1)S(1)}, bf16[1248,768]{1,0:T(8,128)(2,1)}, u32[]{:S(2)}) copy-start(bf16[1248,768]{1,0:T(8,128)(2,1)} %get-tuple-element.34) | copy-start | bytes 5750788
  229.7 139.8 %reduce-scatter.17.cloned.1.call-start = ((), (), s32[]{:S(2)}) async-start(), calls=%async_computation.10 | async-start | bytes 5308416 | tf_op jit(solution)/shard_map/reduce_scatter | solution.py:467
  240.7 130.8 %all-to-all-start.1 = ((bf16[4,192,384]{2,1,0:T(8,128)(2,1)}), bf16[4,192,384]{2,1,0:T(8,128)(2,1)S(1)}, u32[]{:S(2)}, u32[]{:S(2)}) async-start(bf16[4,192,384]{2,1,0:T(8,128)(2,1)} %bitcast.63), calls=%async_computation.4 | async-start | bytes 1179648 | tf_op jit(solution)/shard_map/all_to_all | solution.py:479
  246.0 24.7 %copy-start.7 = (f32[8,768]{1,0:T(8,128)S(1)}, f32[8,768]{1,0:T(8,128)}, u32[]{:S(2)}) copy-start(f32[8,768]{1,0:T(8,128)} %get-tuple-element.36) | copy-start | bytes 73732
  246.0 146.6 %reduce-scatter.21.cloned.1.call-start = ((), (), s32[]{:S(2)}) async-start(), calls=%async_computation.12 | async-start | bytes 245760
  261.9 156.5 %reduce-scatter.19.cloned.1.call-start = ((), (), s32[]{:S(2)}) async-start(), calls=%async_computation.11 | async-start | bytes 737280
  262.1 114.6 %collective-permute-start.11 = (bf16[2,80,768]{2,1,0:T(8,128)(2,1)S(1)}, bf16[2,80,768]{2,1,0:T(8,128)(2,1)}, u32[]{:S(2)}, u32[]{:S(2)}) collective-permute-start(bf16[2,80,768]{2,1,0:T(8,128)(2,1)S(1)} %bitcast.178), channel_id=1, source_target_pairs={{2,3},{6,7},{10,11},{14,15},{18,19},{22,23},{26,27},{30,31}} | collective-permute-start | bytes 737288 | tf_op jit(solution)/shard_map/ppermute | solution.py:451
  263.5 113.3 %collective-permute-start.10 = (bf16[2,80,768]{2,1,0:T(8,128)(2,1)S(1)}, bf16[2,80,768]{2,1,0:T(8,128)(2,1)}, u32[]{:S(2)}, u32[]{:S(2)}) collective-permute-start(bf16[2,80,768]{2,1,0:T(8,128)(2,1)S(1)} %bitcast.179), channel_id=1, source_target_pairs={{1,3},{5,7},{9,11},{13,15},{17,19},{21,23},{25,27},{29,31}} | collective-permute-start | bytes 737288 | tf_op jit(solution)/shard_map/ppermute | solution.py:451
  264.9 111.9 %collective-permute-start.9 = (bf16[2,80,768]{2,1,0:T(8,128)(2,1)S(1)}, bf16[2,80,768]{2,1,0:T(8,128)(2,1)}, u32[]{:S(2)}, u32[]{:S(2)}) collective-permute-start(bf16[2,80,768]{2,1,0:T(8,128)(2,1)S(1)} %bitcast.180), channel_id=1, source_target_pairs={{0,3},{4,7},{8,11},{12,15},{16,19},{20,23},{24,27},{28,31}} | collective-permute-start | bytes 737288 | tf_op jit(solution)/shard_map/ppermute | solution.py:451
  355.9 20.9 %copy-start.4 = (bf16[2,3,208,768]{3,2,1,0:T(8,128)(2,1)S(1)}, bf16[2,3,208,768]{3,2,1,0:T(8,128)(2,1)}, u32[]{:S(2)}) copy-start(bf16[2,3,208,768]{3,2,1,0:T(8,128)(2,1)} %slice.233) | copy-start | bytes 5750788
  371.4 49.7 %all-to-all-start = ((bf16[4,96,768]{2,1,0:T(8,128)(2,1)}), bf16[4,96,768]{2,1,0:T(8,128)(2,1)S(1)}, u32[]{:S(2)}, u32[]{:S(2)}) async-start(bf16[4,96,768]{2,1,0:T(8,128)(2,1)} %bitcast.144), calls=%async_computation.3 | async-start | bytes 1179648 | tf_op jit(solution)/shard_map/all_to_all | solution.py:478
  (12 other events, 89.7 us)
Sparse Core Ops, SparseCore 0:
  158.0 61.7 reduce-scatter.22
  223.4 36.7 reduce-scatter.14
  263.6 48.0 reduce-scatter.12
  315.1 54.3 reduce-scatter.16
  372.3 20.2 reduce-scatter.20
  394.7 23.7 reduce-scatter.18
